TPU v7x, 32 devices: a whole 2x2x4 slice. The times are simulated.
32 devices in a mesh: groups: 2 (over y), tm: 4 (over z), archive: 2 (over x), replica: 2 (over core).
Axes of the slice: x: 2, y: 2, z: 4, core: 2. Of those that a mesh axis runs over, the one named last changes fastest.
Arguments:
- seeds: float32 [4, 2048, 256], P(('groups', 'archive'), 'tm', 'replica'), parts along dimension 0, may hold values from 0.01 to 1
- band: bfloat16 [4, 16, 3, 128, 128], P(('groups', 'archive'), 'tm'), parts along dimension 0, may hold values from 9.9658966e-05 to 1
- band_mask: int32 [4, 16, 3], P(('groups', 'archive'), 'tm'), parts along dimension 0, may hold values 0 or 1
- recording: int32 [4, 2048], P(('groups', 'archive'), 'tm'), parts along dimension 0, may hold values from 0 to 15, never falling along the last dimension, each value on 1 to 256 neighbouring positions
- cross: bfloat16 [4, 16, 28, 128, 128], P(('groups', 'archive'), 'tm'), parts along dimension 0, may hold values from 9.9658966e-05 to 1
- cross_ref: int32 [4, 16, 28], P(('groups', 'archive'), 'tm'), parts along dimension 0, may hold values from 0 to 31, as said below
- cross_mask: int32 [4, 16, 28], P(('groups', 'archive'), 'tm'), parts along dimension 0, may hold values 0 or 1
Outputs:
- labels: float32 [4, 2048, 256], P(('groups', 'archive'), 'tm', 'replica'), parts along dimension 0
- change: float32 [4], P('groups'), parts along dimension 0
There are 2 independent parts, one for each index of `groups`. A program takes and returns all parts, laid end to end along the dimension named above; each array names one. Nothing has to cross between parts.
Inputs may be any that keep to these rules, and one draw needn't show every extreme that they name: `cross_ref`: the 112 listed blocks of the rows of one index pair of tm and archive lie in the rows of other index pairs, and at most 16 of them lie in the 512 rows of any one such index pair, a bound reached on every device.
All inputs are finite; a program needn't handle non-finite values. No bound on the sum of `band_mask` or of `cross_mask` on one device may be relied on, other than what follows from the above.
Results may differ from a plain program's by a relative error of at most 0.0003.
Values may be sent and summed in bfloat16 or wider, within the bound.
A program may use at most 64 MiB of HBM per device.

v0:
```python
import jax
import jax.numpy as jnp
from jax import lax
from jax.sharding import PartitionSpec as P

ITERS = 2


ALPHA = 0.85


def with_halo(cells, sides, width):
    for axis, dim in sides:
        count = lax.axis_size(axis)
        ends = count - 1
        head = lax.slice_in_dim(cells, 0, width, axis=dim)
        tail = lax.slice_in_dim(cells, cells.shape[dim] - width, cells.shape[dim], axis=dim)
        cells = jnp.concatenate(
            [
                lax.ppermute(tail, axis, [(i, (i + 1) % count) for i in range(ends)]),
                cells,
                lax.ppermute(head, axis, [((i + 1) % count, i) for i in range(ends)]),
            ],
            axis=dim,
        )
    return cells


def shards(seeds, band, band_mask, recording, cross, cross_ref, cross_mask):
    n_arch = lax.axis_size("archive")
    n_tm = lax.axis_size("tm")
    n_rep = lax.axis_size("replica")
    start_labels = seeds[0]
    rows, width = start_labels.shape
    block = band.shape[3]
    nblk = rows // block
    slots = cross_ref.shape[2]
    record = recording[0] + 1
    record_ext = with_halo(record, (("tm", 0),), block)
    ext_blocks = record_ext.reshape(nblk + 2, block)
    near_record = jnp.stack(
        [ext_blocks[0:nblk], ext_blocks[1 : nblk + 1], ext_blocks[2 : nblk + 2]], axis=1
    )
    own_record = record.reshape(nblk, block)
    keep = (own_record[:, None, :, None] == near_record[:, :, None, :]) & (
        band_mask[0][:, :, None, None] > 0
    )
    band_w = jnp.where(keep, band[0], jnp.zeros((), jnp.bfloat16))
    live = cross_mask[0] > 0
    cross_rows = jnp.sum(cross[0], axis=3, dtype=jnp.float32)
    degree = jnp.sum(band_w, axis=(1, 3), dtype=jnp.float32) + jnp.sum(
        jnp.where(live[:, :, None], cross_rows, 0.0), axis=1
    )
    degree = degree.reshape(rows, 1)
    listed = cross_ref[0].reshape(-1)
    arch_blocks = nblk * n_tm
    owner_arch = listed // arch_blocks
    within_arch = listed % arch_blocks
    owner_tm = within_arch // nblk
    local_block = within_arch % nblk
    dest = owner_tm * n_arch + owner_arch
    total = n_tm * n_arch
    peers = total - 1
    cap = (nblk * slots + peers - 1) // peers
    listed_live = live.reshape(-1)
    order = jnp.arange(listed.shape[0])
    rank = jnp.sum((dest[:, None] == dest[None, :]) & (order[None, :] < order[:, None]), axis=1)
    spot = dest * cap + rank
    table = jnp.arange(total * cap)
    request = jnp.sum(
        jnp.where(spot[None, :] == table[:, None], local_block[None, :] + 1, 0), axis=1
    )
    request = request.reshape(total, cap)
    wanted = lax.all_to_all(request, ("tm", "archive"), split_axis=0, concat_axis=0, tiled=True)
    current = start_labels
    changes = []
    count = total * rows * width * n_rep
    for step in range(ITERS):
        rounded = current.astype(jnp.bfloat16)
        extended = with_halo(rounded, (("tm", 0),), block)
        ext_lab = extended.reshape(nblk + 2, block, width)
        near = jnp.stack([ext_lab[0:nblk], ext_lab[1 : nblk + 1], ext_lab[2 : nblk + 2]], axis=1)
        serve = rounded.reshape(nblk, block, width)[jnp.maximum(wanted - 1, 0)]
        returned = lax.all_to_all(serve, ("tm", "archive"), split_axis=0, concat_axis=0, tiled=True)
        fetched = returned.reshape(total * cap, block, width)[spot]
        panels = jnp.where(listed_live[:, None, None], fetched, jnp.zeros((), jnp.bfloat16))
        panels = panels.reshape(nblk, slots, block, width)
        near_sum = jnp.einsum("boij,bojc->bic", band_w, near, preferred_element_type=jnp.float32)
        far_sum = jnp.einsum("bkij,bkjc->bic", cross[0], panels, preferred_element_type=jnp.float32)
        spread = (near_sum + far_sum).reshape(rows, width)
        updated = (1.0 - ALPHA) * start_labels + ALPHA * (current + spread) / (1.0 + degree)
        step_change = jnp.sum(jnp.square(updated - current))
        changes.append(lax.psum(step_change, ("tm", "archive", "replica")) / count)
        current = updated
    change = jnp.stack(changes)
    return (current[None], change)


def solution(mesh):
    return jax.shard_map(
        shards,
        mesh=mesh,
        in_specs=(
            P(("groups", "archive"), "tm", "replica"),
            P(("groups", "archive"), "tm", None, None, None),
            P(("groups", "archive"), "tm", None),
            P(("groups", "archive"), "tm"),
            P(("groups", "archive"), "tm", None, None, None),
            P(("groups", "archive"), "tm", None),
            P(("groups", "archive"), "tm", None),
        ),
        out_specs=(P(("groups", "archive"), "tm", "replica"), P("groups")),
        check_vma=False,
    )
```

profile of v0, /device:TPU:0, one launch (start us, length us, event | category | flops | bytes accessed | tf_op | source)
XLA Modules:
  0.0 270.7 jit_solution(144327052428263949)
XLA Ops:
  0.6 0.8 reshape_squeeze.5
  1.4 0.2 convert_reduce_fusion.2
  1.6 0.1 select_reduce_fusion.1
  1.7 0.7 all_to_all.12
  2.4 7.3 %all-to-all-start = ((s32[8,1,16]{2,1,0:T(1,128)}), s32[8,1,16]{2,1,0:T(1,128)S(1)}, u32[]{:S(2)}, u32[]{:S(2)}) async-start(s32[8,1,16]{2,1,0:T(1,128)} %bitcast.17), calls=%async_computation | async-start | bytes 8192 | tf_op jit(solution)/shard_map/all_to_all | solution.py:74
  9.7 1.0 convert_element_type.38
  10.6 5.4 %all-to-all-done = s32[8,1,16]{2,1,0:T(1,128)S(1)} async-done(((s32[8,1,16]{2,1,0:T(1,128)}), s32[8,1,16]{2,1,0:T(1,128)S(1)}, u32[]{:S(2)}, u32[]{:S(2)}) %all-to-all-start) | async-done | bytes 544 | tf_op jit(solution)/shard_map/all_to_all | solution.py:74
  16.1 0.1 reshape.489
  16.2 3.1 %gather_fusion = bf16[128,128,128]{2,1,0:T(8,128)(2,1)} fusion(bf16[4,128,128]{2,1,0:T(8,128)(2,1)S(1)} %convert_element_type.38, s32[1024]{0:T(1024)S(1)} %pad_clamp_fusion.1), kind=kCustom, calls=%fused_computation | custom fusion | bytes 8389120 | tf_op jit(solution)/shard_map/gather | solution.py:83
  19.2 0.0 copy-start.4
  19.2 0.0 copy-start
  19.2 0.0 copy-start.2
  19.2 0.0 copy-start.3
  19.2 4.7 %all-to-all-start.1 = ((bf16[8,16,128,128]{3,2,1,0:T(8,128)(2,1)}), bf16[8,16,128,128]{3,2,1,0:T(8,128)(2,1)}, u32[]{:S(2)}, u32[]{:S(2)}) async-start(bf16[8,16,128,128]{3,2,1,0:T(8,128)(2,1)} %bitcast.149), calls=%async_computation.1 | async-start | bytes 8388608 | tf_op jit(solution)/shard_map/all_to_all | solution.py:84
  23.9 0.0 copy-done.4
  23.9 0.0 copy-start.5
  23.9 0.0 copy-start.1
  24.0 3.9 %collective-permute-start = (s32[128]{0:T(128)S(1)}, s32[128]{0:T(128)S(1)}, u32[]{:S(2)}, u32[]{:S(2)}) collective-permute-start(s32[128]{0:T(128)S(1)} %get-tuple-element.20), channel_id=1, source_target_pairs={{0,4},{4,8},{8,12},{1,5},{5,9},{9,13},{2,6},{6,10},{10,14},{3,7},{... | collective-permute-start | bytes 1544 | tf_op jit(solution)/shard_map/ppermute | solution.py:20
  27.9 1.3 collective-permute-start.1
  29.2 0.0 copy-done
  29.3 4.5 %collective-permute-start.2 = (bf16[128,128]{1,0:T(8,128)(2,1)S(1)}, bf16[128,128]{1,0:T(8,128)(2,1)S(1)}, u32[]{:S(2)}, u32[]{:S(2)}) collective-permute-start(bf16[128,128]{1,0:T(8,128)(2,1)S(1)} %get-tuple-element.16), channel_id=1, source_target_pairs={{0,4},{4,8},{8,12},{1,5},{5,9},{9,13},{2,6},{6,10},{10,14},{3,7},{... | collective-permute-start | bytes 98312 | tf_op jit(solution)/shard_map/ppermute | solution.py:20
  33.8 1.3 collective-permute-start.3
  35.1 0.0 copy-done.2
  35.1 0.1 reshape_squeeze.6
  35.2 0.0 copy-done.3
  35.2 3.1 %convert_reduce_fusion = f32[4,28,128]{2,1,0:T(8,128)S(1)} fusion(bf16[1,4,28,128,128]{4,3,2,1,0:T(8,128)(2,1)} %param.11), kind=kLoop, calls=%fused_computation.4 | loop fusion | flops 3655680 | bytes 3727360 | tf_op jit(solution)/shard_map/reduce_sum | solution.py:50
  38.3 0.1 select_reduce_fusion
  38.4 0.0 copy-done.5
  38.5 0.1 copy.22
  38.6 52.9 %collective-permute-done = s32[128]{0:T(128)S(1)} collective-permute-done((s32[128]{0:T(128)S(1)}, s32[128]{0:T(128)S(1)}, u32[]{:S(2)}, u32[]{:S(2)}) %collective-permute-start) | collective-permute-done | bytes 544 | tf_op jit(solution)/shard_map/ppermute | solution.py:20
  91.5 0.0 collective-permute-done.1
  91.5 0.0 copy-done.1
  91.5 0.3 convert_reduce_fusion.1
  91.9 0.0 collective-permute-done.2
  91.9 0.0 collective-permute-done.3
  91.9 0.3 convolution_bitcast_fusion.1
  92.2 24.1 %all-to-all-done.1 = bf16[8,16,128,128]{3,2,1,0:T(8,128)(2,1)} async-done(((bf16[8,16,128,128]{3,2,1,0:T(8,128)(2,1)}), bf16[8,16,128,128]{3,2,1,0:T(8,128)(2,1)}, u32[]{:S(2)}, u32[]{:S(2)}) %all-to-all-start.1) | async-done | bytes 4194336 | tf_op jit(solution)/shard_map/all_to_all | solution.py:84
  116.3 5.1 %gather_fusion.1 = bf16[112,128,128]{2,1,0:T(8,128)(2,1)} fusion(bf16[128,128,128]{2,1,0:T(8,128)(2,1)} %bitcast.19, s32[1024]{0:T(1024)S(1)} %pad_clamp_fusion), kind=kCustom, calls=%fused_computation.1 | custom fusion | bytes 7340480 | tf_op jit(solution)/shard_map/gather | solution.py:85
  121.4 4.3 %add_convert_fusion = (bf16[4,128,128]{2,1,0:T(8,128)(2,1)S(1)}, f32[4,128,128]{2,1,0:T(8,128)S(1)}) fusion(f32[4,128,128]{2,1,0:T(8,128)S(1)} %bitcast.152, f32[4,128]{1,0:T(4,128)S(1)} %add_add_fusion, f32[4,128,128]{2,1,0:T(8,128)S(1)} %convolution_bitcast_fusion.1, bf16[4,28,128,128]{3,2,1,0:T(8,128)(2,1)} %bitcast.153, ...), kind=kOutput, calls=%fused_computation.53 | convolution fusion | flops 472055808 | bytes 8259696 | tf_op jit(solution)/shard_map/bkij,bkjc->bic/dot_general | solution.py:89
  125.7 3.0 %gather_fusion.2 = bf16[128,128,128]{2,1,0:T(8,128)(2,1)} fusion(bf16[4,128,128]{2,1,0:T(8,128)(2,1)S(1)} %get-tuple-element.22, s32[1024]{0:T(1024)S(1)} %pad_clamp_fusion.1), kind=kCustom, calls=%fused_computation.2 | custom fusion | bytes 8389120 | tf_op jit(solution)/shard_map/gather | solution.py:83
  128.8 4.6 %all-to-all-start.2 = ((bf16[8,16,128,128]{3,2,1,0:T(8,128)(2,1)}), bf16[8,16,128,128]{3,2,1,0:T(8,128)(2,1)}, u32[]{:S(2)}, u32[]{:S(2)}) async-start(bf16[8,16,128,128]{3,2,1,0:T(8,128)(2,1)} %bitcast.150), calls=%async_computation.2 | async-start | bytes 8388608 | tf_op jit(solution)/shard_map/all_to_all | solution.py:84
  133.3 0.1 fusion.61
  133.5 3.8 %collective-permute-start.4 = (bf16[128,128]{1,0:T(8,128)(2,1)S(1)}, bf16[128,128]{1,0:T(8,128)(2,1)S(1)}, u32[]{:S(2)}, u32[]{:S(2)}) collective-permute-start(bf16[128,128]{1,0:T(8,128)(2,1)S(1)} %get-tuple-element.12), channel_id=1, source_target_pairs={{0,4},{4,8},{8,12},{1,5},{5,9},{9,13},{2,6},{6,10},{10,14},{3,7},{... | collective-permute-start | bytes 98312 | tf_op jit(solution)/shard_map/ppermute | solution.py:20
  137.3 1.3 collective-permute-start.5
  138.6 63.2 %collective-permute-done.4 = bf16[128,128]{1,0:T(8,128)(2,1)S(1)} collective-permute-done((bf16[128,128]{1,0:T(8,128)(2,1)S(1)}, bf16[128,128]{1,0:T(8,128)(2,1)S(1)}, u32[]{:S(2)}, u32[]{:S(2)}) %collective-permute-start.4) | collective-permute-done | bytes 32800 | tf_op jit(solution)/shard_map/ppermute | solution.py:20
  201.8 0.0 collective-permute-done.5
  201.8 0.3 convolution_bitcast_fusion
  202.2 24.8 %all-to-all-done.2 = bf16[8,16,128,128]{3,2,1,0:T(8,128)(2,1)} async-done(((bf16[8,16,128,128]{3,2,1,0:T(8,128)(2,1)}), bf16[8,16,128,128]{3,2,1,0:T(8,128)(2,1)}, u32[]{:S(2)}, u32[]{:S(2)}) %all-to-all-start.2) | async-done | bytes 4194336 | tf_op jit(solution)/shard_map/all_to_all | solution.py:84
  227.0 5.1 %gather_fusion.3 = bf16[112,128,128]{2,1,0:T(8,128)(2,1)} fusion(bf16[128,128,128]{2,1,0:T(8,128)(2,1)} %bitcast.36, s32[1024]{0:T(1024)S(1)} %pad_clamp_fusion), kind=kCustom, calls=%fused_computation.3 | custom fusion | bytes 7340480 | tf_op jit(solution)/shard_map/gather | solution.py:85
  232.0 4.3 %fusion.25 = f32[4,128,128]{2,1,0:T(8,128)S(1)} fusion(f32[4,128,128]{2,1,0:T(8,128)S(1)} %convolution_bitcast_fusion, bf16[4,28,128,128]{3,2,1,0:T(8,128)(2,1)} %bitcast.154, pred[4,28]{1,0:T(4,128)(4,1)S(1)} %compare_bitcast_fusion, bf16[1,4,28,128,128]{4,3,2,1,0:T(8,128)(2,1)} %param.11), kind=kOutput, calls=%fused_computation.20 | convolution fusion | flops 471662592 | bytes 7864432 | tf_op jit(solution)/shard_map/bkij,bkjc->bic/dot_general | solution.py:89
  236.4 0.8 fusion.51
  237.2 30.7 %all-reduce = (f32[]{:T(128)}, f32[]{:T(128)}) all-reduce(f32[]{:T(128)} %get-tuple-element.3, f32[]{:T(128)} %get-tuple-element.2), channel_id=1, replica_groups=mesh['groups'=2,'tm'=4,'archive'=2,'replica'=2] {'tm','archive','replica'}, use_global_device_ids=true, to_apply=%region_8.9 | all-reduce | flops 2 | bytes 16 | tf_op jit(solution)/shard_map/psum | solution.py:93
  269.2 0.6 pad_maximum_fusion.5
  269.8 0.9 fusion.43
  (20 shorter events, 0.2 us)
Async XLA Ops:
  2.4 13.6 %all-to-all-start = ((s32[8,1,16]{2,1,0:T(1,128)}), s32[8,1,16]{2,1,0:T(1,128)S(1)}, u32[]{:S(2)}, u32[]{:S(2)}) async-start(s32[8,1,16]{2,1,0:T(1,128)} %bitcast.17), calls=%async_computation | async-start | bytes 8192 | tf_op jit(solution)/shard_map/all_to_all | solution.py:74
  19.2 4.7 %copy-start.4 = (s32[1,512]{1,0:T(1,128)S(1)}, s32[1,512]{1,0:T(1,128)}, u32[]{:S(2)}) copy-start(s32[1,512]{1,0:T(1,128)} %param.10) | copy-start | bytes 6148
  19.2 10.0 %copy-start = (f32[1,512,128]{2,1,0:T(8,128)S(1)}, f32[1,512,128]{2,1,0:T(8,128)}, u32[]{:S(2)}) copy-start(f32[1,512,128]{2,1,0:T(8,128)} %param.7) | copy-start | bytes 786436
  19.2 15.9 %copy-start.2 = (s32[1,4,28]{2,1,0:T(4,128)S(1)}, s32[1,4,28]{2,1,0:T(4,128)}, u32[]{:S(2)}) copy-start(s32[1,4,28]{2,1,0:T(4,128)} %param.12) | copy-start | bytes 1348
  19.2 16.0 %copy-start.3 = (s32[1,4,28]{2,1,0:T(4,128)S(1)}, s32[1,4,28]{2,1,0:T(4,128)}, u32[]{:S(2)}) copy-start(s32[1,4,28]{2,1,0:T(4,128)} %param.13) | copy-start | bytes 1348
  19.2 97.1 %all-to-all-start.1 = ((bf16[8,16,128,128]{3,2,1,0:T(8,128)(2,1)}), bf16[8,16,128,128]{3,2,1,0:T(8,128)(2,1)}, u32[]{:S(2)}, u32[]{:S(2)}) async-start(bf16[8,16,128,128]{3,2,1,0:T(8,128)(2,1)} %bitcast.149), calls=%async_computation.1 | async-start | bytes 8388608 | tf_op jit(solution)/shard_map/all_to_all | solution.py:84
  23.9 14.5 %copy-start.5 = (s32[1,4,3]{1,0,2:T(1,128)S(1)}, s32[1,4,3]{1,0,2:T(1,128)}, u32[]{:S(2)}) copy-start(s32[1,4,3]{1,0,2:T(1,128)} %param.9) | copy-start | bytes 148
  23.9 67.6 %copy-start.1 = (bf16[1,4,3,128,128]{4,3,2,1,0:T(8,128)(2,1)S(1)}, bf16[1,4,3,128,128]{4,3,2,1,0:T(8,128)(2,1)}, u32[]{:S(2)}) copy-start(bf16[1,4,3,128,128]{4,3,2,1,0:T(8,128)(2,1)} %param.8) | copy-start | bytes 1179652
  24.0 67.5 %collective-permute-start = (s32[128]{0:T(128)S(1)}, s32[128]{0:T(128)S(1)}, u32[]{:S(2)}, u32[]{:S(2)}) collective-permute-start(s32[128]{0:T(128)S(1)} %get-tuple-element.20), channel_id=1, source_target_pairs={{0,4},{4,8},{8,12},{1,5},{5,9},{9,13},{2,6},{6,10},{10,14},{3,7},{... | collective-permute-start | bytes 1544 | tf_op jit(solution)/shard_map/ppermute | solution.py:20
  27.9 63.6 %collective-permute-start.1 = (s32[128]{0:T(128)S(1)}, s32[128]{0:T(128)S(1)}, u32[]{:S(2)}, u32[]{:S(2)}) collective-permute-start(s32[128]{0:T(128)S(1)} %get-tuple-element.21), channel_id=1, source_target_pairs={{4,0},{8,4},{12,8},{5,1},{9,5},{13,9},{6,2},{10,6},{14,10},{7,3},{... | collective-permute-start | bytes 1544 | tf_op jit(solution)/shard_map/ppermute | solution.py:22
  29.3 62.6 %collective-permute-start.2 = (bf16[128,128]{1,0:T(8,128)(2,1)S(1)}, bf16[128,128]{1,0:T(8,128)(2,1)S(1)}, u32[]{:S(2)}, u32[]{:S(2)}) collective-permute-start(bf16[128,128]{1,0:T(8,128)(2,1)S(1)} %get-tuple-element.16), channel_id=1, source_target_pairs={{0,4},{4,8},{8,12},{1,5},{5,9},{9,13},{2,6},{6,10},{10,14},{3,7},{... | collective-permute-start | bytes 98312 | tf_op jit(solution)/shard_map/ppermute | solution.py:20
  33.8 58.0 %collective-permute-start.3 = (bf16[128,128]{1,0:T(8,128)(2,1)S(1)}, bf16[128,128]{1,0:T(8,128)(2,1)S(1)}, u32[]{:S(2)}, u32[]{:S(2)}) collective-permute-start(bf16[128,128]{1,0:T(8,128)(2,1)S(1)} %get-tuple-element.17), channel_id=1, source_target_pairs={{4,0},{8,4},{12,8},{5,1},{9,5},{13,9},{6,2},{10,6},{14,10},{7,3},{... | collective-permute-start | bytes 98312 | tf_op jit(solution)/shard_map/ppermute | solution.py:22
  128.8 98.2 %all-to-all-start.2 = ((bf16[8,16,128,128]{3,2,1,0:T(8,128)(2,1)}), bf16[8,16,128,128]{3,2,1,0:T(8,128)(2,1)}, u32[]{:S(2)}, u32[]{:S(2)}) async-start(bf16[8,16,128,128]{3,2,1,0:T(8,128)(2,1)} %bitcast.150), calls=%async_computation.2 | async-start | bytes 8388608 | tf_op jit(solution)/shard_map/all_to_all | solution.py:84
  133.5 68.3 %collective-permute-start.4 = (bf16[128,128]{1,0:T(8,128)(2,1)S(1)}, bf16[128,128]{1,0:T(8,128)(2,1)S(1)}, u32[]{:S(2)}, u32[]{:S(2)}) collective-permute-start(bf16[128,128]{1,0:T(8,128)(2,1)S(1)} %get-tuple-element.12), channel_id=1, source_target_pairs={{0,4},{4,8},{8,12},{1,5},{5,9},{9,13},{2,6},{6,10},{10,14},{3,7},{... | collective-permute-start | bytes 98312 | tf_op jit(solution)/shard_map/ppermute | solution.py:20
  137.3 64.5 %collective-permute-start.5 = (bf16[128,128]{1,0:T(8,128)(2,1)S(1)}, bf16[128,128]{1,0:T(8,128)(2,1)S(1)}, u32[]{:S(2)}, u32[]{:S(2)}) collective-permute-start(bf16[128,128]{1,0:T(8,128)(2,1)S(1)} %get-tuple-element.13), channel_id=1, source_target_pairs={{4,0},{8,4},{12,8},{5,1},{9,5},{13,9},{6,2},{10,6},{14,10},{7,3},{... | collective-permute-start | bytes 98312 | tf_op jit(solution)/shard_map/ppermute | solution.py:22
where the time goes:
time: 271 us
  waiting for transfers between devices  170 us (63%)
  starting transfers between devices  32.6 us (12%)
  blocking collectives  30.7 us (11%)
  local copies, waits for them, and re-layouts  18 us (7%)
  matrix products  9.32 us (3%)
  other arithmetic  7.38 us (3%)
    ppermute x3, waiting for transfers between devices, with_halo(): lax.ppermute(tail, axis, [(i, (i + 1) % count) for i in range(ends)])  116 us
    all_to_all x2, waiting for transfers between devices, shards(): lax.all_to_all(serve, ('tm', 'archive'), split_axis=0, concat_axis=0, til...  48.9 us
    psum x1, blocking collectives, shards(): changes.append(lax.psum(step_change, ('tm', 'archive', 'replica')) / count)  30.7 us
    ppermute x3, starting transfers between devices, with_halo(): lax.ppermute(tail, axis, [(i, (i + 1) % count) for i in range(ends)])  12.3 us
    gather x2, local copies, waits for them, and re-layouts, shards(): fetched = returned.reshape(total * cap, block, width)[spot]  10.1 us
    all_to_all x2, starting transfers between devices, shards(): lax.all_to_all(serve, ('tm', 'archive'), split_axis=0, concat_axis=0, til...  9.25 us
    dot_general x2, matrix products, shards(): jnp.einsum('bkij,bkjc->bic', cross[0], panels, preferred_element_type=jnp...  8.67 us
    all_to_all x1, starting transfers between devices, shards(): lax.all_to_all(request, ('tm', 'archive'), split_axis=0, concat_axis=0, t...  7.25 us
  transfers between devices with their start and end apart: 9, of which 5 were waited for; matrix products, arithmetic and copies ran while one was open for 2% of the time, Pallas kernels for 0%

commit v1 on v0

v1 whole, which is shorter than its diff:
```python
import functools

import jax
import jax.numpy as jnp
from jax import lax
from jax.experimental import pallas as pl
from jax.experimental.pallas import tpu as pltpu
from jax.sharding import PartitionSpec as P

ITERS = 2
ALPHA = 0.85


def each(lo, hi, body):
    if hi - lo <= 4:
        for i in range(lo, hi):
            body(i)
    else:
        lax.fori_loop(lo, hi, lambda i, c: (body(i), c)[1], 0)


def kernel(
    dims,
    seeds,
    band,
    band_mask,
    recording,
    cross,
    cross_ref,
    cross_mask,
    out,
    change,
    lab0,
    lab1,
    cross_v,
    band_v,
    rec_s,
    rec_halo,
    current,
    scale,
    chg,
    in_sem,
    zs,
    zr,
    xs,
    xr,
    rs,
    rr,
    cs,
    cr,
    out_sem,
):
    n_tm, n_arch, n_rep, nblk, block, slots, nsub, group = dims
    labs = (lab0, lab1)
    per = nblk // nsub
    t = lax.axis_index("tm")
    a = lax.axis_index("archive")
    r = lax.axis_index("replica")
    total = n_tm * n_arch * n_rep
    me = (t * n_arch + a) * n_rep + r
    zero_slot = n_arch * n_tm * nblk
    own = (a * n_tm + t) * nblk
    archive_lo = a * n_tm * nblk
    archive_hi = archive_lo + n_tm * nblk - 1
    MESH = pl.DeviceIdType.MESH

    def peer(step):
        other = lax.rem(me + step, total)
        return {
            "tm": other // (n_arch * n_rep),
            "archive": lax.rem(other // n_rep, n_arch),
            "replica": lax.rem(other, n_rep),
        }

    loads = [pltpu.make_async_copy(band.at[0], band_v, in_sem.at[0])]
    for b in range(nblk):
        loads.append(pltpu.make_async_copy(cross.at[0, b], cross_v.at[b], in_sem.at[1 + b]))

    rec_halo[...] = jnp.full(rec_halo.shape, -1, jnp.int32)

    barrier = pltpu.get_barrier_semaphore()

    def greet(step):
        pl.semaphore_signal(barrier, inc=1, device_id=peer(step), device_id_type=MESH)

    each(1, total, greet)
    for b in range(nblk):
        rec_s[b] = jnp.broadcast_to(recording[:, b * block : (b + 1) * block], (8, block))
        lab0[own + b] = seeds[0, b * block : (b + 1) * block, :].astype(jnp.bfloat16)
    zeros = jnp.zeros((block, lab0.shape[2]), jnp.bfloat16)
    lab0[zero_slot] = zeros
    lab1[zero_slot] = zeros
    for load in loads:
        load.start()
    pl.semaphore_wait(barrier, total - 1)

    def z_copy(it, d, j, sub):
        src = t - j if d == 0 else t + j
        nxt = lax.rem(t + 1, n_tm) if d == 0 else lax.rem(t + n_tm - 1, n_tm)
        lab = labs[it]
        where = pl.ds((a * n_tm + src) * nblk + sub * per, per)
        return pltpu.make_async_remote_copy(
            src_ref=lab.at[where],
            dst_ref=lab.at[where],
            send_sem=zs.at[it, d, j, sub],
            recv_sem=zr.at[it, d, j + 1, sub],
            device_id={"tm": nxt},
            device_id_type=MESH,
        )

    def z_arrive(it, d, j, sub):
        src = t - j if d == 0 else t + j
        lab = labs[it]
        where = pl.ds((a * n_tm + src) * nblk + sub * per, per)
        return pltpu.make_async_remote_copy(
            src_ref=lab.at[where],
            dst_ref=lab.at[where],
            send_sem=zs.at[it, d, j, sub],
            recv_sem=zr.at[it, d, j, sub],
            device_id={"tm": lax.rem(t + 1, n_tm)},
            device_id_type=MESH,
        )

    def x_copy(it, m, src, sub):
        lab = labs[it]
        where = pl.ds((a * n_tm + src) * nblk + sub * per, per)
        return pltpu.make_async_remote_copy(
            src_ref=lab.at[where],
            dst_ref=lab.at[where],
            send_sem=xs.at[it, m, src, sub],
            recv_sem=xr.at[it, m, src, sub],
            device_id={"archive": lax.rem(a + m, n_arch)},
            device_id_type=MESH,
        )

    def x_arrive(it, m, src, sub):
        lab = labs[it]
        frm = lax.rem(a + n_arch - m, n_arch)
        where = pl.ds((frm * n_tm + src) * nblk + sub * per, per)
        return pltpu.make_async_remote_copy(
            src_ref=lab.at[where],
            dst_ref=lab.at[where],
            send_sem=xs.at[it, m, src, sub],
            recv_sem=xr.at[it, m, src, sub],
            device_id={"archive": lax.rem(a + m, n_arch)},
            device_id_type=MESH,
        )

    def has_next(d):
        return t + 1 < n_tm if d == 0 else t >= 1

    def has_source(d, j):
        return t >= j if d == 0 else t + j < n_tm

    def own_send(it, sub):
        for d in range(2):
            pl.when(has_next(d))(lambda d=d: z_copy(it, d, 0, sub).start())
        each(1, n_arch, lambda m: x_copy(it, m, t, sub).start())

    def hand_on(it, j, sub):
        for d in range(2):

            @pl.when(has_source(d, j))
            def _():
                src = t - j if d == 0 else t + j
                z_arrive(it, d, j, sub).wait_recv()
                pl.when(has_next(d))(lambda: z_copy(it, d, j, sub).start())
                each(1, n_arch, lambda m: x_copy(it, m, src, sub).start())

    def x_wait(it):
        def one(src):
            for sub in range(nsub):
                each(1, n_arch, lambda m: x_arrive(it, m, src, sub).wait_recv())

        each(0, n_tm, one)

    def drain(it):
        def one(src):
            for sub in range(nsub):
                each(1, n_arch, lambda m: x_copy(it, m, src, sub).wait_send())

        each(0, n_tm, one)

        def hop(j):
            for d in range(2):
                go = has_next(d) & has_source(d, j)

                @pl.when(go)
                def _():
                    for sub in range(nsub):
                        z_copy(it, d, j, sub).wait_send()

        each(0, n_tm, hop)

    def rec_copy(d):
        return pltpu.make_async_remote_copy(
            src_ref=rec_s.at[nblk - 1 if d == 0 else 0],
            dst_ref=rec_halo.at[d],
            send_sem=rs.at[d],
            recv_sem=rr.at[d],
            device_id={"tm": lax.rem(t + 1, n_tm) if d == 0 else lax.rem(t + n_tm - 1, n_tm)},
            device_id_type=MESH,
        )

    for d in range(2):
        pl.when(has_next(d))(lambda d=d: rec_copy(d).start())
    for sub in range(nsub):
        own_send(0, sub)

    def rows(b):
        return pl.ds(b * block, block)


    def cross_degree(b):
        loads[1 + b].wait()
        acc = jnp.zeros((block, block), jnp.float32)
        for k in range(slots):
            live = (cross_mask[0, b, k] > 0).astype(jnp.float32)
            acc += cross_v[b, k].astype(jnp.float32) * live
        scale[rows(b), :] = acc

    def band_weights(b):
        acc = scale[rows(b), :]
        mine = jnp.broadcast_to(rec_s[b, 0:1, :], (block, block)).astype(jnp.float32).T
        for o in range(3):
            near = b + o - 1
            if near < 0:
                theirs = rec_halo[0, 0:1, :]
            elif near >= nblk:
                theirs = rec_halo[1, 0:1, :]
            else:
                theirs = rec_s[near, 0:1, :]
            theirs = jnp.where(band_mask[0, b, o] > 0, theirs, -2).astype(jnp.float32)
            w = jnp.where(mine == theirs, band_v[b, o].astype(jnp.float32), 0.0)
            band_v[b, o] = w.astype(jnp.bfloat16)
            acc += w
        degree = jnp.sum(acc, axis=1, keepdims=True)
        scale[rows(b), :] = jnp.broadcast_to(ALPHA / (1.0 + degree), (block, scale.shape[1]))

    def spread_of(it, b):
        lab = labs[it]
        near = [jnp.clip(own + b + o - 1, archive_lo, archive_hi) for o in range(3)]
        acc = jnp.dot(
            jnp.concatenate([band_v[b, o] for o in range(3)], axis=1),
            jnp.concatenate([lab[i] for i in near], axis=0),
            preferred_element_type=jnp.float32,
        )
        for k0 in range(0, slots, group):
            ks = range(k0, k0 + group)
            spots = [jnp.where(cross_mask[0, b, k] > 0, cross_ref[0, b, k], zero_slot) for k in ks]
            acc += jnp.dot(
                jnp.concatenate([cross_v[b, k] for k in ks], axis=1),
                jnp.concatenate([lab[i] for i in spots], axis=0),
                preferred_element_type=jnp.float32,
            )
        return acc

    def step(it, b):
        spread = spread_of(it, b)
        first = seeds[0, rows(b), :]
        before = first if it == 0 else current[rows(b), :]
        updated = (1.0 - ALPHA) * first + (before + spread) * scale[rows(b), :]
        current[rows(b), :] = updated
        if it + 1 < ITERS:
            labs[it + 1][own + b] = updated.astype(jnp.bfloat16)
        diff = updated - before
        return jnp.sum(diff * diff, axis=0, keepdims=True)

    work = [functools.partial(cross_degree, b) for b in range(nblk)]
    for j_sub in range(nsub):
        if work:
            work.pop(0)()
        hand_on(0, 1, j_sub)
    for f in work:
        f()
    for d in range(2):
        came = has_source(d, 1)
        pl.when(came)(lambda d=d: rec_copy(d).wait_recv())
    loads[0].wait()
    work = [functools.partial(band_weights, b) for b in range(nblk)]

    def later(it, lo):
        def one(j):
            for sub in range(nsub):
                hand_on(it, j, sub)

        each(lo, n_tm, one)

    if n_tm > 2 and n_tm <= 6:
        for sub in range(nsub):
            hand_on(0, 2, sub)
            if work:
                work.pop(0)()
        for f in work:
            f()
        later(0, 3)
    else:
        for f in work:
            f()
        later(0, 2)
    x_wait(0)

    sums = jnp.zeros((1, seeds.shape[2]), jnp.float32)
    for sub in range(nsub):
        for b in range(sub * per, (sub + 1) * per):
            sums += step(0, b)
        own_send(1, sub)
        if sub >= 1:
            hand_on(1, 1, sub - 1)
    hand_on(1, 1, nsub - 1)
    later(1, 2)
    x_wait(1)
    totals = [sums]
    sums = jnp.zeros((1, seeds.shape[2]), jnp.float32)
    writes = []
    for b in range(nblk):
        sums += step(1, b)
        writes.append(
            pltpu.make_async_copy(current.at[rows(b)], out.at[0, rows(b)], out_sem.at[b])
        )
        writes[-1].start()
    totals.append(sums)

    row = lax.broadcasted_iota(jnp.int32, (8, seeds.shape[2]), 0)
    chg[me] = jnp.where(row == 0, totals[0], jnp.where(row == 1, totals[1], 0.0))

    def chg_copy(s):
        return pltpu.make_async_remote_copy(
            src_ref=chg.at[me],
            dst_ref=chg.at[me],
            send_sem=cs.at[s],
            recv_sem=cr.at[s],
            device_id=peer(s),
            device_id_type=MESH,
        )

    def chg_arrive(s):
        frm = lax.rem(me + total - s, total)
        return pltpu.make_async_remote_copy(
            src_ref=chg.at[frm],
            dst_ref=chg.at[frm],
            send_sem=cs.at[s],
            recv_sem=cr.at[s],
            device_id=peer(s),
            device_id_type=MESH,
        )

    each(1, total, lambda s: chg_copy(s).start())
    for it in range(ITERS):
        drain(it)
    for d in range(2):
        pl.when(has_next(d))(lambda d=d: rec_copy(d).wait_send())
    for write in writes:
        write.wait()
    each(1, total, lambda s: chg_arrive(s).wait_recv())
    everyone = jnp.sum(chg[...], axis=0)
    share = 1.0 / (n_tm * n_arch * n_rep * nblk * block * seeds.shape[2])
    for it in range(ITERS):
        change[it] = jnp.sum(everyone[it : it + 1, :]) * share
    each(1, total, lambda s: chg_copy(s).wait_send())


def shards(seeds, band, band_mask, recording, cross, cross_ref, cross_mask):
    n_arch = lax.axis_size("archive")
    n_tm = lax.axis_size("tm")
    n_rep = lax.axis_size("replica")
    _, rows, width = seeds.shape
    nblk, block = band.shape[1], band.shape[3]
    slots = cross_ref.shape[2]
    nsub = nblk if n_tm * n_arch <= 16 else 1
    group = max(g for g in (4, 3, 2, 1) if slots % g == 0)
    total = n_tm * n_arch * n_rep
    held = (n_arch * n_tm * nblk + 1, block, width)
    need = 2 * held[0] * block * width * 2 + cross.size * 2 + band.size * 2 + 4 * seeds.size * 4
    need += total * 8 * width * 4
    dma = pltpu.SemaphoreType.DMA
    vmem = pl.BlockSpec(memory_space=pltpu.VMEM)
    smem = pl.BlockSpec(memory_space=pltpu.SMEM)
    hbm = pl.BlockSpec(memory_space=pl.ANY)
    labels, change = pl.pallas_call(
        functools.partial(kernel, (n_tm, n_arch, n_rep, nblk, block, slots, nsub, group)),
        out_shape=(
            jax.ShapeDtypeStruct(seeds.shape, jnp.float32),
            jax.ShapeDtypeStruct((ITERS,), jnp.float32),
        ),
        in_specs=[vmem, hbm, smem, vmem, hbm, smem, smem],
        out_specs=(hbm, smem),
        scratch_shapes=[
            pltpu.VMEM(held, jnp.bfloat16),
            pltpu.VMEM(held, jnp.bfloat16),
            pltpu.VMEM(cross.shape[1:], jnp.bfloat16),
            pltpu.VMEM(band.shape[1:], jnp.bfloat16),
            pltpu.VMEM((nblk, 8, block), jnp.int32),
            pltpu.VMEM((2, 8, block), jnp.int32),
            pltpu.VMEM((rows, width), jnp.float32),
            pltpu.VMEM((rows, width), jnp.float32),
            pltpu.VMEM((total, 8, width), jnp.float32),
            dma((1 + nblk,)),
            dma((ITERS, 2, n_tm + 1, nsub)),
            dma((ITERS, 2, n_tm + 1, nsub)),
            dma((ITERS, n_arch, n_tm, nsub)),
            dma((ITERS, n_arch, n_tm, nsub)),
            dma((2,)),
            dma((2,)),
            dma((total,)),
            dma((total,)),
            dma((nblk,)),
        ],
        compiler_params=pltpu.CompilerParams(
            collective_id=0,
            has_side_effects=True,
            vmem_limit_bytes=need + (8 << 20),
        ),
    )(seeds, band, band_mask, recording, cross, cross_ref, cross_mask)
    return labels, change


def solution(mesh):
    return jax.shard_map(
        shards,
        mesh=mesh,
        in_specs=(
            P(("groups", "archive"), "tm", "replica"),
            P(("groups", "archive"), "tm", None, None, None),
            P(("groups", "archive"), "tm", None),
            P(("groups", "archive"), "tm"),
            P(("groups", "archive"), "tm", None, None, None),
            P(("groups", "archive"), "tm", None),
            P(("groups", "archive"), "tm", None),
        ),
        out_specs=(P(("groups", "archive"), "tm", "replica"), P("groups")),
        check_vma=False,
    )
```

time: 271 us -> 54.9 us (0.20)
  waiting for transfers between devices: 170 us -> 0 us
  Pallas kernels: 0 us -> 46 us
  starting transfers between devices: 32.6 us -> 0 us
  blocking collectives: 30.7 us -> 0 us
  local copies, waits for them, and re-layouts: 18 us -> 8.01 us
  matrix products: 9.32 us -> 0 us
  other arithmetic: 7.38 us -> 0 us
    ppermute x6 -> x0, waiting for transfers between devices: 116 us -> none  [the longest x3 116 us: with_halo(): lax.ppermute(tail, axis, [(i, (i + 1) % count) for i in range(ends)])]
    all_to_all x3 -> x0, waiting for transfers between devices: 54.3 us -> none  [the longest x2 48.9 us: shards(): lax.all_to_all(serve, ('tm', 'archive'), split_axis=0, concat_axis=0, til...]
    pallas_call x0 -> x1, Pallas kernels: none -> 46 us  [shards(): pl.pallas_call(functools.partial(kernel, (n_tm, n_arch, n_rep, nblk, bloc...]
    psum x1 -> x0, blocking collectives: 30.7 us -> none  [shards(): changes.append(lax.psum(step_change, ('tm', 'archive', 'replica')) / count)]
    all_to_all x3 -> x0, starting transfers between devices: 16.5 us -> none  [the longest x2 9.25 us: shards(): lax.all_to_all(serve, ('tm', 'archive'), split_axis=0, concat_axis=0, til...]
    gather x4 -> x0, local copies, waits for them, and re-layouts: 16.2 us -> none  [the longest x2 10.1 us: shards(): fetched = returned.reshape(total * cap, block, width)[spot]]
    ppermute x6 -> x0, starting transfers between devices: 16.1 us -> none  [the longest x3 12.3 us: with_halo(): lax.ppermute(tail, axis, [(i, (i + 1) % count) for i in range(ends)])]
    dot_general x4 -> x0, matrix products: 9.32 us -> none  [the longest x2 8.67 us: shards(): jnp.einsum('bkij,bkjc->bic', cross[0], panels, preferred_element_type=jnp...]
  transfers between devices with their start and end apart: 9 -> 0, of which waited for: 5 -> 0; matrix products, arithmetic and copies ran while one was open for 2% -> 0% of each run, Pallas kernels for 0% -> 0%
where the time goes in v1:
time: 54.9 us; the launch traced here: 54.6 us
  Pallas kernels  46 us (84%)
  local copies, waits for them, and re-layouts  8.01 us (15%)
  between operations  0.64 us (1%)
    pallas_call x1, Pallas kernels, shards(): pl.pallas_call(functools.partial(kernel, (n_tm, n_arch, n_rep, nblk, bloc...  46 us
    unnamed x15, local copies, waits for them, and re-layouts  8.01 us

profile of v1, /device:TPU:0, one launch (start us, length us, event | category | flops | bytes accessed | tf_op | source)
XLA Modules:
  0.0 54.6 jit_solution(12737732794439040036)
XLA Ops:
  0.6 0.8 %copy.9.band_mask = s32[1,4,3]{2,1,0:T(4,128)S(1)} copy(s32[1,4,3]{1,0,2:T(1,128)} %param.9) | data formatting | bytes 96 | tf_op args[2]
  1.4 0.0 copy-start
  1.4 2.0 %copy-done = bf16[1,4,28,128,128]{4,3,2,1,0:T(8,128)(2,1)S(1)} copy-done((bf16[1,4,28,128,128]{4,3,2,1,0:T(8,128)(2,1)S(1)}, bf16[1,4,28,128,128]{4,3,2,1,0:T(8,128)(2,1)}, u32[]{:S(2)}) %copy-start) | copy-done | bytes 3670040
  3.4 0.0 copy-start.1
  3.4 1.0 %copy-done.1 = bf16[1,4,3,128,128]{4,3,2,1,0:T(8,128)(2,1)S(1)} copy-done((bf16[1,4,3,128,128]{4,3,2,1,0:T(8,128)(2,1)S(1)}, bf16[1,4,3,128,128]{4,3,2,1,0:T(8,128)(2,1)}, u32[]{:S(2)}) %copy-start.1) | copy-done | bytes 393240
  4.4 0.0 copy-start.2
  4.4 0.9 %copy-done.2 = f32[1,512,128]{2,1,0:T(8,128)S(1)} copy-done((f32[1,512,128]{2,1,0:T(8,128)S(1)}, f32[1,512,128]{2,1,0:T(8,128)}, u32[]{:S(2)}) %copy-start.2) | copy-done | bytes 262168
  5.4 0.0 copy-start.3
  5.4 0.7 %copy-done.3 = s32[1,512]{1,0:T(1,128)S(1)} copy-done((s32[1,512]{1,0:T(1,128)S(1)}, s32[1,512]{1,0:T(1,128)}, u32[]{:S(2)}) %copy-start.3) | copy-done | bytes 2072
  6.1 0.0 copy-start.4
  6.1 0.7 %copy-done.4 = s32[1,4,28]{2,1,0:T(4,128)S(1)} copy-done((s32[1,4,28]{2,1,0:T(4,128)S(1)}, s32[1,4,28]{2,1,0:T(4,128)}, u32[]{:S(2)}) %copy-start.4) | copy-done | bytes 472
  6.7 0.0 copy-start.5
  6.7 0.7 %copy-done.5 = s32[1,4,28]{2,1,0:T(4,128)S(1)} copy-done((s32[1,4,28]{2,1,0:T(4,128)S(1)}, s32[1,4,28]{2,1,0:T(4,128)}, u32[]{:S(2)}) %copy-start.5) | copy-done | bytes 472
  7.4 46.0 %shard_map.86 = (f32[1,512,128]{2,1,0:T(8,128)S(1)}, f32[2]{0:T(128)S(1)}) custom-call(f32[1,512,128]{2,1,0:T(8,128)S(1)} %copy-done.2, bf16[1,4,3,128,128]{4,3,2,1,0:T(8,128)(2,1)S(1)} %copy-done.1, s32[1,4,3]{2,1,0:T(4,128)S(1)} %copy.9.band_mask, s32[1,512]{1,0:T(1,128)S(1)} %copy-done.3, bf16[1,4,28,128,128]{4,3,2,1,0:T(8,128)(2,1)S(1)} %copy-done, ...), custom_call_target="tpu_custom_call" | custom-call | tf_op jit(solution)/shard_map/pallas_call | solution.py:380
  53.4 0.7 %copy.12 = f32[1,512,128]{2,1,0:T(8,128)} copy(f32[1,512,128]{2,1,0:T(8,128)S(1)} %get-tuple-element.4) | data formatting | bytes 524288
  54.1 0.5 copy.13
Async XLA Ops:
  1.4 2.0 %copy-start = (bf16[1,4,28,128,128]{4,3,2,1,0:T(8,128)(2,1)S(1)}, bf16[1,4,28,128,128]{4,3,2,1,0:T(8,128)(2,1)}, u32[]{:S(2)}) copy-start(bf16[1,4,28,128,128]{4,3,2,1,0:T(8,128)(2,1)} %cross.1) | copy-start | bytes 11010052
  3.4 1.0 %copy-start.1 = (bf16[1,4,3,128,128]{4,3,2,1,0:T(8,128)(2,1)S(1)}, bf16[1,4,3,128,128]{4,3,2,1,0:T(8,128)(2,1)}, u32[]{:S(2)}) copy-start(bf16[1,4,3,128,128]{4,3,2,1,0:T(8,128)(2,1)} %band.1) | copy-start | bytes 1179652
  4.4 0.9 %copy-start.2 = (f32[1,512,128]{2,1,0:T(8,128)S(1)}, f32[1,512,128]{2,1,0:T(8,128)}, u32[]{:S(2)}) copy-start(f32[1,512,128]{2,1,0:T(8,128)} %seeds.1) | copy-start | bytes 786436
  5.4 0.7 %copy-start.3 = (s32[1,512]{1,0:T(1,128)S(1)}, s32[1,512]{1,0:T(1,128)}, u32[]{:S(2)}) copy-start(s32[1,512]{1,0:T(1,128)} %recording.1) | copy-start | bytes 6148
  6.1 0.7 %copy-start.4 = (s32[1,4,28]{2,1,0:T(4,128)S(1)}, s32[1,4,28]{2,1,0:T(4,128)}, u32[]{:S(2)}) copy-start(s32[1,4,28]{2,1,0:T(4,128)} %cross_ref.1) | copy-start | bytes 1348
  6.7 0.7 %copy-start.5 = (s32[1,4,28]{2,1,0:T(4,128)S(1)}, s32[1,4,28]{2,1,0:T(4,128)}, u32[]{:S(2)}) copy-start(s32[1,4,28]{2,1,0:T(4,128)} %cross_mask.1) | copy-start | bytes 1348

commit v2 on v1

--- a/solution.py
+++ b/solution.py
@@ -12,7 +12,7 @@
 
 
 def each(lo, hi, body):
-    if hi - lo <= 4:
+    if hi - lo <= 16:
         for i in range(lo, hi):
             body(i)
     else:
@@ -21,15 +21,20 @@
 
 def kernel(
     dims,
+    seeds_in,
+    band,
+    band_mask_in,
+    recording_in,
+    cross,
+    cross_ref_in,
+    cross_mask_in,
+    out,
+    change,
     seeds,
-    band,
+    recording,
     band_mask,
-    recording,
-    cross,
     cross_ref,
     cross_mask,
-    out,
-    change,
     lab0,
     lab1,
     cross_v,
@@ -44,13 +49,15 @@
     zr,
     xs,
     xr,
+    ds,
+    dr_sem,
     rs,
     rr,
     cs,
     cr,
     out_sem,
 ):
-    n_tm, n_arch, n_rep, nblk, block, slots, nsub, group = dims
+    n_tm, n_arch, n_rep, nblk, block, slots, nsub, group, half = dims
     labs = (lab0, lab1)
     per = nblk // nsub
     t = lax.axis_index("tm")
@@ -64,14 +71,30 @@
     archive_hi = archive_lo + n_tm * nblk - 1
     MESH = pl.DeviceIdType.MESH
 
+    def wrap(i, n):
+        return jnp.where(i >= n, i - n, i)
+
+    def offsets(step):
+        return step // (n_arch * n_rep), (step // n_rep) % n_arch, step % n_rep
+
     def peer(step):
-        other = lax.rem(me + step, total)
-        return {
-            "tm": other // (n_arch * n_rep),
-            "archive": lax.rem(other // n_rep, n_arch),
-            "replica": lax.rem(other, n_rep),
-        }
-
+        dt, da, dr = offsets(step)
+        return {"tm": wrap(t + dt, n_tm), "archive": wrap(a + da, n_arch), "replica": wrap(r + dr, n_rep)}
+
+    small = [
+        pltpu.make_async_copy(src, dst, in_sem.at[1 + nblk + i])
+        for i, (src, dst) in enumerate(
+            (
+                (seeds_in, seeds),
+                (recording_in, recording),
+                (band_mask_in, band_mask),
+                (cross_ref_in, cross_ref),
+                (cross_mask_in, cross_mask),
+            )
+        )
+    ]
+    for load in small:
+        load.start()
     loads = [pltpu.make_async_copy(band.at[0], band_v, in_sem.at[0])]
     for b in range(nblk):
         loads.append(pltpu.make_async_copy(cross.at[0, b], cross_v.at[b], in_sem.at[1 + b]))
@@ -84,19 +107,21 @@
         pl.semaphore_signal(barrier, inc=1, device_id=peer(step), device_id_type=MESH)
 
     each(1, total, greet)
+    for load in loads:
+        load.start()
+    small[0].wait()
+    small[1].wait()
     for b in range(nblk):
         rec_s[b] = jnp.broadcast_to(recording[:, b * block : (b + 1) * block], (8, block))
         lab0[own + b] = seeds[0, b * block : (b + 1) * block, :].astype(jnp.bfloat16)
     zeros = jnp.zeros((block, lab0.shape[2]), jnp.bfloat16)
     lab0[zero_slot] = zeros
     lab1[zero_slot] = zeros
-    for load in loads:
-        load.start()
     pl.semaphore_wait(barrier, total - 1)
 
     def z_copy(it, d, j, sub):
         src = t - j if d == 0 else t + j
-        nxt = lax.rem(t + 1, n_tm) if d == 0 else lax.rem(t + n_tm - 1, n_tm)
+        nxt = jnp.minimum(t + 1, n_tm - 1) if d == 0 else jnp.maximum(t - 1, 0)
         lab = labs[it]
         where = pl.ds((a * n_tm + src) * nblk + sub * per, per)
         return pltpu.make_async_remote_copy(
@@ -117,7 +142,7 @@
             dst_ref=lab.at[where],
             send_sem=zs.at[it, d, j, sub],
             recv_sem=zr.at[it, d, j, sub],
-            device_id={"tm": lax.rem(t + 1, n_tm)},
+            device_id={"tm": wrap(t + 1, n_tm)},
             device_id_type=MESH,
         )
 
@@ -129,20 +154,20 @@
             dst_ref=lab.at[where],
             send_sem=xs.at[it, m, src, sub],
             recv_sem=xr.at[it, m, src, sub],
-            device_id={"archive": lax.rem(a + m, n_arch)},
+            device_id={"archive": wrap(a + m, n_arch)},
             device_id_type=MESH,
         )
 
     def x_arrive(it, m, src, sub):
         lab = labs[it]
-        frm = lax.rem(a + n_arch - m, n_arch)
+        frm = wrap(a + n_arch - m, n_arch)
         where = pl.ds((frm * n_tm + src) * nblk + sub * per, per)
         return pltpu.make_async_remote_copy(
             src_ref=lab.at[where],
             dst_ref=lab.at[where],
             send_sem=xs.at[it, m, src, sub],
             recv_sem=xr.at[it, m, src, sub],
-            device_id={"archive": lax.rem(a + m, n_arch)},
+            device_id={"archive": wrap(a + m, n_arch)},
             device_id_type=MESH,
         )
 
@@ -151,6 +176,57 @@
 
     def has_source(d, j):
         return t >= j if d == 0 else t + j < n_tm
+
+    last = n_tm - 1
+    at_end = (t == 0) | (t == last)
+
+    def direct(src, sub):
+        if sub >= half:
+            return None
+        far = jnp.where((t == 0) | (t == 2), last, 0)
+        return src != far
+
+    def guarded(cond, body):
+        if cond is None:
+            body()
+        else:
+            pl.when(cond)(body)
+
+    def detour(it, kind, sub, arriving):
+        if arriving:
+            src = jnp.where((t == 0) | (t == 2), last, 0)
+        elif kind == 0:
+            src = t
+        else:
+            src = jnp.where(t == 1, last, 0)
+        lab = labs[it]
+        where = pl.ds(((1 - a) * n_tm + src) * nblk + sub * per, per)
+        return pltpu.make_async_remote_copy(
+            src_ref=lab.at[where],
+            dst_ref=lab.at[where],
+            send_sem=ds.at[it, kind, sub],
+            recv_sem=dr_sem.at[it, kind, sub],
+            device_id={"tm": jnp.where(t < 2, 1 - t, 5 - t)},
+            device_id_type=MESH,
+        )
+
+    def sends_kind(kind):
+        return at_end if kind == 0 else jnp.logical_not(at_end)
+
+    def detour_send(it, kind):
+        for sub in range(half):
+
+            @pl.when(sends_kind(kind))
+            def _():
+                src = t if kind == 0 else jnp.where(t == 1, last, 0)
+                x_arrive(it, 1, src, sub).wait_recv()
+                detour(it, kind, sub, False).start()
+
+    def x_send(it, src, sub):
+        guarded(
+            direct(src, sub),
+            lambda: each(1, n_arch, lambda m: x_copy(it, m, src, sub).start()),
+        )
 
     def own_send(it, sub):
         for d in range(2):
@@ -158,26 +234,36 @@
         each(1, n_arch, lambda m: x_copy(it, m, t, sub).start())
 
     def hand_on(it, j, sub):
-        for d in range(2):
+        for d in (1, 0):
 
             @pl.when(has_source(d, j))
             def _():
                 src = t - j if d == 0 else t + j
                 z_arrive(it, d, j, sub).wait_recv()
                 pl.when(has_next(d))(lambda: z_copy(it, d, j, sub).start())
-                each(1, n_arch, lambda m: x_copy(it, m, src, sub).start())
+                x_send(it, src, sub)
 
     def x_wait(it):
         def one(src):
             for sub in range(nsub):
+                if sub < half and src in (0, last):
+                    continue
                 each(1, n_arch, lambda m: x_arrive(it, m, src, sub).wait_recv())
 
         each(0, n_tm, one)
+        for sub in range(half):
+            for kind in range(2):
+                pl.when(sends_kind(1 - kind))(
+                    lambda kind=kind: detour(it, kind, sub, True).wait_recv()
+                )
 
     def drain(it):
         def one(src):
             for sub in range(nsub):
-                each(1, n_arch, lambda m: x_copy(it, m, src, sub).wait_send())
+                guarded(
+                    direct(src, sub),
+                    lambda: each(1, n_arch, lambda m: x_copy(it, m, src, sub).wait_send()),
+                )
 
         each(0, n_tm, one)
 
@@ -191,6 +277,11 @@
                         z_copy(it, d, j, sub).wait_send()
 
         each(0, n_tm, hop)
+        for sub in range(half):
+            for kind in range(2):
+                pl.when(sends_kind(kind))(
+                    lambda kind=kind: detour(it, kind, sub, False).wait_send()
+                )
 
     def rec_copy(d):
         return pltpu.make_async_remote_copy(
@@ -198,7 +289,7 @@
             dst_ref=rec_halo.at[d],
             send_sem=rs.at[d],
             recv_sem=rr.at[d],
-            device_id={"tm": lax.rem(t + 1, n_tm) if d == 0 else lax.rem(t + n_tm - 1, n_tm)},
+            device_id={"tm": jnp.minimum(t + 1, n_tm - 1) if d == 0 else jnp.maximum(t - 1, 0)},
             device_id_type=MESH,
         )
 
@@ -206,6 +297,8 @@
         pl.when(has_next(d))(lambda d=d: rec_copy(d).start())
     for sub in range(nsub):
         own_send(0, sub)
+    for load in small[2:]:
+        load.wait()
 
     def rows(b):
         return pl.ds(b * block, block)
@@ -230,7 +323,7 @@
                 theirs = rec_halo[1, 0:1, :]
             else:
                 theirs = rec_s[near, 0:1, :]
-            theirs = jnp.where(band_mask[0, b, o] > 0, theirs, -2).astype(jnp.float32)
+            theirs = jnp.where(band_mask[o, 0, b] > 0, theirs, -2).astype(jnp.float32)
             w = jnp.where(mine == theirs, band_v[b, o].astype(jnp.float32), 0.0)
             band_v[b, o] = w.astype(jnp.bfloat16)
             acc += w
@@ -266,18 +359,14 @@
         diff = updated - before
         return jnp.sum(diff * diff, axis=0, keepdims=True)
 
+    def neighbours():
+        loads[0].wait()
+        for d in range(2):
+            pl.when(has_source(d, 1))(lambda d=d: rec_copy(d).wait_recv())
+
     work = [functools.partial(cross_degree, b) for b in range(nblk)]
-    for j_sub in range(nsub):
-        if work:
-            work.pop(0)()
-        hand_on(0, 1, j_sub)
-    for f in work:
-        f()
-    for d in range(2):
-        came = has_source(d, 1)
-        pl.when(came)(lambda d=d: rec_copy(d).wait_recv())
-    loads[0].wait()
-    work = [functools.partial(band_weights, b) for b in range(nblk)]
+    work.append(neighbours)
+    work += [functools.partial(band_weights, b) for b in range(nblk)]
 
     def later(it, lo):
         def one(j):
@@ -286,17 +375,24 @@
 
         each(lo, n_tm, one)
 
-    if n_tm > 2 and n_tm <= 6:
+    def do(count):
+        for _ in range(min(count, len(work))):
+            work.pop(0)()
+
+    do(2)
+    for sub in range(nsub):
+        hand_on(0, 1, sub)
+        do(1)
+    detour_send(0, 0)
+    if n_tm == 4:
         for sub in range(nsub):
             hand_on(0, 2, sub)
-            if work:
-                work.pop(0)()
-        for f in work:
-            f()
+            do(2)
+        detour_send(0, 1)
+        do(len(work))
         later(0, 3)
     else:
-        for f in work:
-            f()
+        do(len(work))
         later(0, 2)
     x_wait(0)
 
@@ -308,7 +404,14 @@
         if sub >= 1:
             hand_on(1, 1, sub - 1)
     hand_on(1, 1, nsub - 1)
-    later(1, 2)
+    detour_send(1, 0)
+    if n_tm == 4:
+        for sub in range(nsub):
+            hand_on(1, 2, sub)
+        detour_send(1, 1)
+        later(1, 3)
+    else:
+        later(1, 2)
     x_wait(1)
     totals = [sums]
     sums = jnp.zeros((1, seeds.shape[2]), jnp.float32)
@@ -335,7 +438,9 @@
         )
 
     def chg_arrive(s):
-        frm = lax.rem(me + total - s, total)
+        dt, da, dr = offsets(s)
+        frm = wrap(t + n_tm - dt, n_tm) * n_arch + wrap(a + n_arch - da, n_arch)
+        frm = frm * n_rep + wrap(r + n_rep - dr, n_rep)
         return pltpu.make_async_remote_copy(
             src_ref=chg.at[frm],
             dst_ref=chg.at[frm],
@@ -367,25 +472,29 @@
     _, rows, width = seeds.shape
     nblk, block = band.shape[1], band.shape[3]
     slots = cross_ref.shape[2]
-    nsub = nblk if n_tm * n_arch <= 16 else 1
+    nsub = 2 if n_tm * n_arch <= 16 and nblk % 2 == 0 else 1
+    half = 0
     group = max(g for g in (4, 3, 2, 1) if slots % g == 0)
     total = n_tm * n_arch * n_rep
+    band_mask = jnp.transpose(band_mask, (2, 0, 1))
     held = (n_arch * n_tm * nblk + 1, block, width)
-    need = 2 * held[0] * block * width * 2 + cross.size * 2 + band.size * 2 + 4 * seeds.size * 4
-    need += total * 8 * width * 4
     dma = pltpu.SemaphoreType.DMA
-    vmem = pl.BlockSpec(memory_space=pltpu.VMEM)
     smem = pl.BlockSpec(memory_space=pltpu.SMEM)
     hbm = pl.BlockSpec(memory_space=pl.ANY)
     labels, change = pl.pallas_call(
-        functools.partial(kernel, (n_tm, n_arch, n_rep, nblk, block, slots, nsub, group)),
+        functools.partial(kernel, (n_tm, n_arch, n_rep, nblk, block, slots, nsub, group, half)),
         out_shape=(
             jax.ShapeDtypeStruct(seeds.shape, jnp.float32),
             jax.ShapeDtypeStruct((ITERS,), jnp.float32),
         ),
-        in_specs=[vmem, hbm, smem, vmem, hbm, smem, smem],
+        in_specs=[hbm] * 7,
         out_specs=(hbm, smem),
         scratch_shapes=[
+            pltpu.VMEM(seeds.shape, jnp.float32),
+            pltpu.VMEM(recording.shape, jnp.int32),
+            pltpu.SMEM(band_mask.shape, jnp.int32),
+            pltpu.SMEM(cross_ref.shape, jnp.int32),
+            pltpu.SMEM(cross_mask.shape, jnp.int32),
             pltpu.VMEM(held, jnp.bfloat16),
             pltpu.VMEM(held, jnp.bfloat16),
             pltpu.VMEM(cross.shape[1:], jnp.bfloat16),
@@ -395,11 +504,13 @@
             pltpu.VMEM((rows, width), jnp.float32),
             pltpu.VMEM((rows, width), jnp.float32),
             pltpu.VMEM((total, 8, width), jnp.float32),
-            dma((1 + nblk,)),
+            dma((6 + nblk,)),
             dma((ITERS, 2, n_tm + 1, nsub)),
             dma((ITERS, 2, n_tm + 1, nsub)),
             dma((ITERS, n_arch, n_tm, nsub)),
             dma((ITERS, n_arch, n_tm, nsub)),
+            dma((ITERS, 2, nsub)),
+            dma((ITERS, 2, nsub)),
             dma((2,)),
             dma((2,)),
             dma((total,)),
@@ -409,7 +520,7 @@
         compiler_params=pltpu.CompilerParams(
             collective_id=0,
             has_side_effects=True,
-            vmem_limit_bytes=need + (8 << 20),
+            vmem_limit_bytes=63 << 20,
         ),
     )(seeds, band, band_mask, recording, cross, cross_ref, cross_mask)
     return labels, change

time: 54.9 us -> 45.5 us (0.83)
  local copies, waits for them, and re-layouts: 8.01 us -> 2.8 us
  Pallas kernels: 46 us -> 41.9 us
    unnamed x15 -> x2, local copies, waits for them, and re-layouts: 8.01 us -> 2.8 us
    pallas_call x1, Pallas kernels: 46 us -> 41.9 us  [shards(): pl.pallas_call(functools.partial(kernel, (n_tm, n_arch, n_rep, nblk, bloc...]
where the time goes in v2:
time: 45.5 us; the launch traced here: 45.4 us
  Pallas kernels  41.9 us (92%)
  local copies, waits for them, and re-layouts  2.8 us (6%)
  between operations  0.64 us (1%)
    pallas_call x1, Pallas kernels, shards(): pl.pallas_call(functools.partial(kernel, (n_tm, n_arch, n_rep, nblk, bloc...  41.9 us
    unnamed x2, local copies, waits for them, and re-layouts  2.8 us

profile of v2, /device:TPU:0, one launch (start us, length us, event | category | flops | bytes accessed | tf_op | source)
XLA Modules:
  0.0 45.4 jit_solution(11384513630223258313)
XLA Ops:
  0.6 41.9 %shard_map.86 = (f32[1,512,128]{2,1,0:T(8,128)}, f32[2]{0:T(128)}) custom-call(f32[1,512,128]{2,1,0:T(8,128)} %seeds_in.1, bf16[1,4,3,128,128]{4,3,2,1,0:T(8,128)(2,1)} %band.1, s32[3,1,4]{2,1,0:T(1,128)} %bitcast.1, s32[1,512]{1,0:T(1,128)} %recording_in.1, bf16[1,4,28,128,128]{4,3,2,1,0:T(8,128)(2,1)} %cross.1, s32[1,4,28]{2,1,0:T(4,128)} %cross_ref_in.1, ...), custom_call_target="tpu_custom_call" | custom-call | tf_op jit(solution)/shard_map/pallas_call | solution.py:484
  42.6 1.7 %copy.11 = f32[1,512,128]{2,1,0:T(8,128)} copy(f32[1,512,128]{2,1,0:T(8,128)} %get-tuple-element.4) | data formatting | bytes 524288
  44.2 1.1 %copy.12 = f32[2]{0:T(128)} copy(f32[2]{0:T(128)} %get-tuple-element.5) | data formatting | bytes 16

commit v3 on v2

--- a/solution.py
+++ b/solution.py
@@ -412,6 +412,7 @@
         later(1, 3)
     else:
         later(1, 2)
+    drain(0)
     x_wait(1)
     totals = [sums]
     sums = jnp.zeros((1, seeds.shape[2]), jnp.float32)
@@ -451,8 +452,7 @@
         )
 
     each(1, total, lambda s: chg_copy(s).start())
-    for it in range(ITERS):
-        drain(it)
+    drain(1)
     for d in range(2):
         pl.when(has_next(d))(lambda d=d: rec_copy(d).wait_send())
     for write in writes:

time: 45.5 us -> 45.5 us (level)
  no operation moved by 1% of the time
where the time goes in v3:
time: 45.5 us; the launch traced here: 45.4 us
  Pallas kernels  41.9 us (92%)
  local copies, waits for them, and re-layouts  2.8 us (6%)
  between operations  0.64 us (1%)
    pallas_call x1, Pallas kernels, shards(): pl.pallas_call(functools.partial(kernel, (n_tm, n_arch, n_rep, nblk, bloc...  41.9 us
    unnamed x2, local copies, waits for them, and re-layouts  2.8 us

profile of v3, /device:TPU:0, one launch (start us, length us, event | category | flops | bytes accessed | tf_op | source)
XLA Modules:
  0.0 45.4 jit_solution(4824353181581805650)
XLA Ops:
  0.6 41.9 %shard_map.86 = (f32[1,512,128]{2,1,0:T(8,128)}, f32[2]{0:T(128)}) custom-call(f32[1,512,128]{2,1,0:T(8,128)} %seeds_in.1, bf16[1,4,3,128,128]{4,3,2,1,0:T(8,128)(2,1)} %band.1, s32[3,1,4]{2,1,0:T(1,128)} %bitcast.1, s32[1,512]{1,0:T(1,128)} %recording_in.1, bf16[1,4,28,128,128]{4,3,2,1,0:T(8,128)(2,1)} %cross.1, s32[1,4,28]{2,1,0:T(4,128)} %cross_ref_in.1, ...), custom_call_target="tpu_custom_call" | custom-call | tf_op jit(solution)/shard_map/pallas_call | solution.py:484
  42.6 1.7 %copy.11 = f32[1,512,128]{2,1,0:T(8,128)} copy(f32[1,512,128]{2,1,0:T(8,128)} %get-tuple-element.4) | data formatting | bytes 524288
  44.2 1.1 %copy.12 = f32[2]{0:T(128)} copy(f32[2]{0:T(128)} %get-tuple-element.5) | data formatting | bytes 16
